TPU v7x, 512 devices: a whole 4x8x8 slice. The times are simulated.
512 devices in a mesh: sec: 4 (over z_lo, core), sp: 128 (over x, z_hi, y).
Axes of the slice: x: 4, y: 8, z: 8 (z_hi: 4, z_lo: 2; z = z_hi * 2 + z_lo), core: 2. Of those that a mesh axis runs over, the one named last changes fastest.
Arguments:
- queries: bfloat16 [10240, 4096], P('sp', 'sec'), may hold values from -30 to 30
- keys: bfloat16 [12288, 4096], P('sp', 'sec'), may hold values from -30 to 30
- values: bfloat16 [12288, 4096], P('sp', 'sec'), may hold values from -6 to 6
- query_positions: int32 [3, 10240], P(None, 'sp'), may hold values from 0 to 255, as said below
- key_positions: int32 [3, 12288], P(None, 'sp'), may hold values from 0 to 255, as said below
- mixing: bfloat16 [4096, 64], P('sec'), may hold values from -6 to 6
- kernel: bfloat16 [432, 384], replicated, may hold values from -0.3125 to 0.3125
- bias: float32 [384], replicated, may hold values from -1 to 1
- cache: bfloat16 [2, 128, 2, 40, 16], P(None, 'sp'), may hold values from -6 to 6
Outputs:
- decoded: bfloat16 [4, 128, 2, 40, 384], P('sec', 'sp')
Inputs may be any that keep to these rules, and one draw needn't show every extreme that they name: `key_positions`: rows are the time, row and column positions of packed tokens. `query_positions`: the positions of the last 10240 tokens of key_positions, in order.
All inputs are finite; a program needn't handle non-finite values.
Results may differ from a plain program's by a relative error of at most 0.009.
Values may be sent and summed in bfloat16 or wider, within the bound.
No kernel may reach another device: no remote copies, remote signals or barrier semaphores. Data moves between devices by JAX's collectives and lax.ppermute only.
A program may use at most 64 MiB of HBM per device.

v0:
```python
import math

import jax
import jax.numpy as jnp
import numpy as np
from jax import lax
from jax.experimental import pallas as pl
from jax.experimental.pallas import tpu as pltpu
from jax.sharding import Mesh
from jax.sharding import PartitionSpec as P

HD = 128
STRIP = 24
HEADS_SEC = 8
Q_OWN = 80
K_OWN = 96
V_ROWS = K_OWN // 2
KV_ROWS = K_OWN + V_ROWS
OWN_ROWS = KV_ROWS + Q_OWN + STRIP
MIX = 64
GRID_W = 80
HALF_W = GRID_W // 2
FRAME = 2560
KEYS_PART = 3072
Q_BLOCK = 640
ROWS_BLOCK = Q_BLOCK // GRID_W
SUB = 640
MSG = 4 * GRID_W + 32
TILE_W = 20
C_OUT = 384
SP = ("x", "zh", "y")
MIB = 1024 * 1024
HERE = pl.BlockSpec(memory_space=pltpu.VMEM)


def frequency_row():
    sixth = HD // 6
    time_pairs = (HD - 4 * sixth) // 2
    time = 10000.0 ** (-np.arange(time_pairs) / time_pairs)
    space = 10000.0 ** (-np.arange(sixth) / sixth)
    pairs = np.concatenate([time, space, space])
    return np.repeat(pairs, 2).astype(np.float32)[None, :]


def row_order():
    order = np.zeros((2, 2 * MIX, MIX), np.float32)
    for ch in range(16):
        for ab in range(4):
            for side in range(2):
                order[side, side * MIX + ab * 16 + ch, ch * 4 + ab] = 1.0
    return order


def patch_order():
    pick = np.zeros((2, STRIP, 40), np.float32)
    place = np.zeros((2, MIX, HD), np.float32)
    for side in range(2):
        for patch in range(TILE_W):
            pick[side, patch, 2 * patch + side] = 1.0
        for line in range(4):
            for ch in range(16):
                place[side, line * 16 + ch, line * 32 + side * 16 + ch] = 1.0
    return pick, place


def cosine_sine(angle):
    turns = jnp.floor(angle * jnp.float32(2.0 / math.pi) + 0.5)
    rest = angle - turns * jnp.float32(1.5703125)
    rest = rest - turns * jnp.float32(4.837512969970703e-4)
    rest = rest - turns * jnp.float32(7.549789948768648e-8)
    square = rest * rest
    sine = rest + rest * square * (
        jnp.float32(-1.6666654611e-1) + square * (jnp.float32(8.3321608736e-3) - square * jnp.float32(1.9515295891e-4))
    )
    cosine = 1.0 - 0.5 * square + square * square * (
        jnp.float32(4.166664568298827e-2)
        + square * (jnp.float32(-1.388731625493765e-3) + square * jnp.float32(2.443315711809948e-5))
    )
    quarter = turns.astype(jnp.int32)
    odd = (quarter & 1) == 1
    first, second = jnp.where(odd, sine, cosine), jnp.where(odd, cosine, sine)
    first = jnp.where(((quarter + 1) & 2) == 2, -first, first)
    return first, jnp.where((quarter & 2) == 2, -second, second)


def turn_tables(positions, freq):
    count = positions.shape[1]
    spot = positions.astype(jnp.float32)
    same = lax.broadcasted_iota(jnp.int32, (count, count), 0) == lax.broadcasted_iota(jnp.int32, (count, count), 1)
    column = [jnp.sum(jnp.where(same, spot[i : i + 1], 0.0), axis=1, keepdims=True) for i in range(3)]
    lane = lax.broadcasted_iota(jnp.int32, (count, HD), 1)
    base = jnp.where(lane < 44, column[0], jnp.where(lane < 86, column[1], column[2]))
    angle = base * freq
    cosine, sine = cosine_sine(angle)
    even = lax.rem(lane, 2) == 0
    zero = jnp.zeros_like(sine)
    return cosine, jnp.where(even, -sine, zero), jnp.where(even, zero, sine)


def turn(vectors, tables):
    cosine, from_next, from_last = tables
    wide = vectors.astype(jnp.float32)
    out = wide * cosine + pltpu.roll(wide, HD - 1, 1) * from_next + pltpu.roll(wide, 1, 1) * from_last
    return out.astype(jnp.bfloat16)


def prepare_kernel(qpos, kpos, freq, order, pick, place, queries, keys, values, mixing, cache, out):
    q_tables = turn_tables(qpos[...], freq[...])
    k_tables = turn_tables(kpos[...], freq[...])
    tile = jnp.zeros((STRIP, HD), jnp.float32)
    for side in range(2):
        column = lax.dot_general(
            pick[side], cache[...], (((1,), (1,)), ((), ())), preferred_element_type=jnp.float32
        )
        tile = tile + jnp.dot(column.astype(jnp.bfloat16), place[side], preferred_element_type=jnp.float32)
    tile = tile.astype(jnp.bfloat16)
    mixed = [
        jnp.dot(order[side], mixing[...], preferred_element_type=jnp.float32).astype(jnp.bfloat16)
        for side in range(2)
    ]
    for head in range(HEADS_SEC):
        cols = slice(head * HD, (head + 1) * HD)
        out[head, 0:K_OWN, :] = turn(keys[:, cols], k_tables)
        value = values[:, cols]
        mix_low = lax.dot_general(
            value[:V_ROWS], mixed[0][:, cols], (((1,), (1,)), ((), ())), preferred_element_type=jnp.float32
        )
        mix_high = lax.dot_general(
            value[V_ROWS:], mixed[1][:, cols], (((1,), (1,)), ((), ())), preferred_element_type=jnp.float32
        )
        out[head, K_OWN:KV_ROWS, :] = (mix_low + mix_high).astype(jnp.bfloat16)
        out[head, KV_ROWS : KV_ROWS + Q_OWN, :] = turn(queries[:, cols], q_tables)
        out[head, KV_ROWS + Q_OWN : OWN_ROWS, :] = tile


def prepare(qpos, kpos, queries, keys, values, mixing, cache):
    return pl.pallas_call(
        prepare_kernel,
        in_specs=[HERE] * 11,
        out_specs=HERE,
        out_shape=jax.ShapeDtypeStruct((HEADS_SEC, OWN_ROWS, HD), jnp.bfloat16),
        compiler_params=pltpu.CompilerParams(vmem_limit_bytes=56 * MIB),
        cost_estimate=pl.CostEstimate(flops=50000000, bytes_accessed=1200000, transcendentals=0),
        name="prepare",
    )(
        qpos,
        kpos,
        jnp.asarray(frequency_row()),
        jnp.asarray(row_order(), jnp.bfloat16),
        *(jnp.asarray(part, jnp.bfloat16) for part in patch_order()),
        queries,
        keys,
        values,
        mixing.T,
        cache.transpose(0, 1, 2, 4, 3).reshape(MIX, 40),
    )


def spread_kernel(own, queries, pairs, tiles):
    for part in range(HEADS_SEC):
        lines = own[part, KV_ROWS : KV_ROWS + Q_OWN, :]
        for copy in range(4):
            queries[copy, part] = lines
        pairs[part] = own[part, 0:KV_ROWS, :]
        tiles[part] = own[part, KV_ROWS + Q_OWN : OWN_ROWS, :]


def spread(own):
    return pl.pallas_call(
        spread_kernel,
        in_specs=[HERE],
        out_specs=[HERE] * 3,
        out_shape=[
            jax.ShapeDtypeStruct((4, HEADS_SEC, Q_OWN, HD), jnp.bfloat16),
            jax.ShapeDtypeStruct((HEADS_SEC, KV_ROWS, HD), jnp.bfloat16),
            jax.ShapeDtypeStruct((HEADS_SEC, STRIP, HD), jnp.bfloat16),
        ],
        compiler_params=pltpu.CompilerParams(vmem_limit_bytes=4 * MIB),
        cost_estimate=pl.CostEstimate(flops=0, bytes_accessed=800000, transcendentals=0),
        name="spread",
    )(own)


def add_heads_kernel(parts, out):
    total = parts[0].astype(jnp.float32)
    for part in range(1, 8):
        total = total + parts[part].astype(jnp.float32)
    total = total.astype(jnp.bfloat16)
    for copy in range(4):
        out[copy] = total


def add_heads(parts):
    return pl.pallas_call(
        add_heads_kernel,
        in_specs=[HERE],
        out_specs=HERE,
        out_shape=jax.ShapeDtypeStruct((4, 4, STRIP, HD), jnp.bfloat16),
        compiler_params=pltpu.CompilerParams(vmem_limit_bytes=4 * MIB),
        cost_estimate=pl.CostEstimate(flops=100000, bytes_accessed=300000, transcendentals=0),
        name="add_heads",
    )(parts)


def attend_kernel(*refs):
    q_ref, kv_refs, o_ref = refs[0], refs[1:6], refs[6]
    k_buf, v_buf, s_even, s_odd, levels = refs[7:]
    lane = lax.broadcasted_iota(jnp.int32, (V_ROWS, HD), 1)
    ones = jnp.where(lane == MIX, 1.0, 0.0)
    at = 0
    for kv_ref in kv_refs:
        for part in range(kv_ref.shape[0]):
            k_buf[at : at + K_OWN] = kv_ref[part, 0:K_OWN, :]
            both = kv_ref[part, K_OWN:KV_ROWS, :].astype(jnp.float32)
            v_buf[at : at + V_ROWS] = jnp.where(lane < MIX, both, ones).astype(jnp.bfloat16)
            other = pltpu.roll(both, MIX, 1)
            v_buf[at + V_ROWS : at + K_OWN] = jnp.where(lane < MIX, other, ones).astype(jnp.bfloat16)
            at += K_OWN

    scale = jnp.float32(math.log2(math.e) / math.sqrt(HD))
    diagonal = lax.broadcasted_iota(jnp.int32, (GRID_W, HD), 1) == lax.broadcasted_iota(jnp.int32, (GRID_W, HD), 0)
    low_lane = lax.broadcasted_iota(jnp.int32, (HALF_W, HD), 1) < MIX

    def score(start, rows):
        return lax.dot_general(
            q_ref[start : start + rows, :],
            k_buf[...],
            (((1,), (1,)), ((), ())),
            preferred_element_type=jnp.float32,
        )

    def finish(start, rows, s_ref):
        scores = s_ref[0:rows]
        top = jnp.max(scores, axis=1, keepdims=True)
        weights = jnp.exp2((scores - top) * scale).astype(jnp.bfloat16)
        sums = jnp.dot(weights, v_buf[...], preferred_element_type=jnp.float32)
        total = sums[:, MIX : MIX + 1]
        mean = sums / total
        level = top * scale + jnp.log2(total)
        for block in range(rows // (2 * GRID_W)):
            piece, pair = divmod(start // (2 * GRID_W) + block, 4)
            lines = []
            for half in range(2):
                at = (2 * block + half) * GRID_W
                low = mean[at : at + HALF_W]
                high = pltpu.roll(mean[at + HALF_W : at + GRID_W], MIX, 1)
                lines.append(jnp.where(low_lane, low, high))
                line = jnp.sum(jnp.where(diagonal, level[at : at + GRID_W], 0.0), axis=0, keepdims=True)
                first = line.astype(jnp.bfloat16).astype(jnp.float32)
                line = line - first
                second = line.astype(jnp.bfloat16).astype(jnp.float32)
                third = line - second
                spot = piece * 8 + half * 4
                levels[pair, spot : spot + 4] = jnp.concatenate(
                    [first, second, third, jnp.zeros((1, HD), jnp.float32)], axis=0
                )
            o_ref[pair, piece * GRID_W : (piece + 1) * GRID_W] = jnp.concatenate(lines, axis=0).astype(jnp.bfloat16)

    blocks = [(0, 320), (320, 640), (960, 640), (1600, 640), (2240, 320)]
    buffers = [s_even, s_odd]
    s_even[0:320] = score(0, 320)
    for index, (start, rows) in enumerate(blocks):
        if index + 1 < len(blocks):
            after, count = blocks[index + 1]
            buffers[(index + 1) % 2][0:count] = score(after, count)
        finish(start, rows, buffers[index % 2])
    o_ref[:, 4 * GRID_W : MSG] = levels[...].astype(jnp.bfloat16)


def attend(queries, pairs):
    return pl.pallas_call(
        attend_kernel,
        in_specs=[HERE] * 6,
        out_specs=HERE,
        out_shape=jax.ShapeDtypeStruct((4, MSG, HD), jnp.bfloat16),
        scratch_shapes=[
            pltpu.VMEM((KEYS_PART, HD), jnp.bfloat16),
            pltpu.VMEM((KEYS_PART, HD), jnp.bfloat16),
            pltpu.VMEM((SUB, KEYS_PART), jnp.float32),
            pltpu.VMEM((SUB, KEYS_PART), jnp.float32),
            pltpu.VMEM((4, 32, HD), jnp.float32),
        ],
        compiler_params=pltpu.CompilerParams(vmem_limit_bytes=42 * MIB),
        cost_estimate=pl.CostEstimate(flops=4 * FRAME * KEYS_PART * HD, bytes_accessed=2000000, transcendentals=0),
        name="attend",
    )(queries.reshape(FRAME, HD), *pairs)


def combine_kernel(r_ref, o_ref):
    shares = r_ref.shape[0]
    lane = lax.broadcasted_iota(jnp.int32, (HALF_W, HD), 1)
    row = lax.broadcasted_iota(jnp.int32, (HALF_W, HD), 0)
    zeros = jnp.zeros((16, HD), jnp.float32)
    low_lane = lax.broadcasted_iota(jnp.int32, (STRIP, HD), 1) < MIX
    lines = []
    asides = [r_ref[share, 4 * GRID_W : MSG].astype(jnp.float32) for share in range(shares)]
    for patch_row in range(ROWS_BLOCK):
        at, spot = patch_row % 2 * HALF_W, patch_row * 4
        blocks = [
            r_ref[share, patch_row // 2 * GRID_W : (patch_row // 2 + 1) * GRID_W].astype(jnp.float32)[at : at + HALF_W]
            for share in range(shares)
        ]
        levels = [a[spot : spot + 1] + a[spot + 1 : spot + 2] + a[spot + 2 : spot + 3] for a in asides]
        top = levels[0]
        for level in levels[1:]:
            top = jnp.maximum(top, level)
        powers = [jnp.exp2(level - top) for level in levels]
        total = powers[0]
        for power in powers[1:]:
            total = total + power
        result = jnp.zeros((HALF_W, HD), jnp.float32)
        for block, power in zip(blocks, powers):
            weight = power / total
            low = jnp.sum(jnp.where(lane == row, weight, 0.0), axis=1, keepdims=True)
            high = jnp.sum(jnp.where(lane == row + HALF_W, weight, 0.0), axis=1, keepdims=True)
            result = result + jnp.where(lane < MIX, low, high) * block
        line = jnp.concatenate([zeros[:1], result, pltpu.roll(result, MIX, 1), zeros], axis=0)
        line = line[: 2 * HALF_W + 16]
        lines.append(line if patch_row % 2 == 0 else pltpu.roll(line, MIX, 1))
    for group in range(4):
        for tile in range(4):
            at = tile * TILE_W
            piece = jnp.where(low_lane, lines[2 * group][at : at + STRIP], lines[2 * group + 1][at : at + STRIP])
            piece = piece.astype(jnp.bfloat16)
            for copy in range(2):
                o_ref[copy * 4 + tile, group] = piece


def combine(received):
    return pl.pallas_call(
        combine_kernel,
        in_specs=[HERE],
        out_specs=HERE,
        out_shape=jax.ShapeDtypeStruct((8, 4, STRIP, HD), jnp.bfloat16),
        compiler_params=pltpu.CompilerParams(vmem_limit_bytes=8 * MIB),
        cost_estimate=pl.CostEstimate(flops=1000000, bytes_accessed=900000, transcendentals=0),
        name="combine",
    )(received)


def convolve_kernel(half, own, near, kernel, bias, o_ref, weights, rows):
    tap = {(0, 0, 1): 0, (0, 1, 0): 1, (0, 1, 1): 2, (1, 0, 0): 0, (1, 0, 1): 1, (1, 1, 0): 2}
    nothing = jnp.zeros((16, C_OUT), jnp.bfloat16)
    at = 0
    for side in range(2):
        for shift in range(2):
            for frame in range(3):
                for line in range(4):
                    for b in range(2):
                        step_x = tap.get((side, shift, b))
                        if line == 0 or step_x is None:
                            weights[at : at + 16] = nothing
                        else:
                            source = ((frame * 3 + line - 1) * 3 + step_x) * 16
                            weights[at : at + 16] = kernel[source : source + 16]
                        at += 16
    lane = lax.broadcasted_iota(jnp.int32, (STRIP, HD), 1)
    low = lane < MIX
    top = half[0] == 0
    lines = ([], [])
    for frame in range(3):
        mine = own[frame].astype(jnp.float32)
        beside = near[frame].astype(jnp.float32)
        mine_turned = pltpu.roll(mine, MIX, 1)
        beside_turned = pltpu.roll(beside, MIX, 1)
        upper = jnp.where(top, jnp.where(low, beside_turned, mine_turned), mine)
        lower = jnp.where(top, mine_turned, beside)
        lines[0].append(upper)
        lines[1].append(jnp.where(lane < 96, pltpu.roll(upper, 96, 1), pltpu.roll(lower, 96, 1)))
    spare = jnp.zeros((8, HD), jnp.float32)
    lines = [[jnp.concatenate([part, spare], axis=0) for part in parts] for parts in lines]
    for side in range(2):
        taps = jnp.concatenate(
            [
                jnp.concatenate([part[side + s : side + s + STRIP] for s in range(2) for part in parts], axis=1)
                for parts in lines
            ],
            axis=0,
        ).astype(jnp.bfloat16)
        size = 6 * HD
        sums = jnp.dot(taps, weights[side * size : (side + 1) * size, :], preferred_element_type=jnp.float32)
        sums = sums + bias[...]
        for a in range(2):
            for part in range(C_OUT // HD):
                block = sums[a * STRIP : a * STRIP + TILE_W, part * HD : (part + 1) * HD]
                rows[part, pl.ds(a * 40 + side, TILE_W, 2), :] = block
    o_ref[...] = jnp.concatenate([rows[part] for part in range(C_OUT // HD)], axis=1).astype(jnp.bfloat16)


def convolve(half, own, near, kernel, bias):
    return pl.pallas_call(
        convolve_kernel,
        in_specs=[pl.BlockSpec(memory_space=pltpu.SMEM)] + [HERE] * 4,
        out_specs=HERE,
        out_shape=jax.ShapeDtypeStruct((80, C_OUT), jnp.bfloat16),
        scratch_shapes=[pltpu.VMEM((12 * HD, C_OUT), jnp.bfloat16), pltpu.VMEM((C_OUT // HD, 80, HD), jnp.float32)],
        compiler_params=pltpu.CompilerParams(vmem_limit_bytes=8 * MIB),
        cost_estimate=pl.CostEstimate(flops=100000000, bytes_accessed=500000, transcendentals=0),
        name="convolve",
    )(half, own, near, kernel, bias)


def from_ahead(value, axis, steps):
    return lax.ppermute(value, axis, [((spot + steps) % 4, spot) for spot in range(4)])


def next_pair(value, axes):
    pairs = [(i, i + 8) for i in range(120) if i % 8 < 4] + [(i, i - 8) for i in range(8, 128) if i % 8 >= 4]
    return lax.ppermute(value, axes, pairs)


def cache_strips(tiles, tile_col):
    wide = tiles.reshape(2, 4, STRIP, HD)[:, :, :TILE_W].reshape(2, GRID_W, HD)
    wide = jnp.pad(wide, ((0, 0), (1, 3), (0, 0)))
    wide = lax.dynamic_slice_in_dim(wide, tile_col * TILE_W, STRIP, 1)
    return wide.reshape(2, STRIP, 2, MIX).transpose(2, 1, 0, 3).reshape(2, STRIP, HD)


def on_device(queries, keys, values, query_positions, key_positions, mixing, kernel, bias, cache):
    sp_index = lax.axis_index(SP)
    section = lax.axis_index("sec")
    half = lax.axis_index("y") // 4
    tile_col = sp_index % 4
    own = prepare(query_positions, key_positions, queries, keys, values, mixing, cache)
    own = lax.all_to_all(own, "y", 0, 0)
    q_copies, kv_own, tiles = spread(own)
    query_all = lax.all_to_all(q_copies, "zh", 0, 0)
    kv_last = from_ahead(kv_own, "x", 3)
    pairs = [kv_own, from_ahead(kv_own, "x", 1), kv_last, from_ahead(kv_own[:4], "x", 2), from_ahead(kv_last[4:], "x", 3)]
    cached = cache_strips(tiles, tile_col)
    query_all, pairs, cached = lax.optimization_barrier((query_all, pairs, cached))
    parts = attend(query_all, pairs)
    shares = lax.all_to_all(parts, "zh", 0, 0)
    tiles = lax.all_to_all(combine(shares), "y", 0, 0)
    strip = lax.all_to_all(add_heads(tiles).reshape(16, STRIP, HD), ("sec", "x"), 0, 0)
    strip = jnp.sum(strip.reshape(4, 4, STRIP, HD).astype(jnp.float32), axis=0).astype(jnp.bfloat16)
    strip = jnp.concatenate([cached, strip], axis=0)
    frames = lax.dynamic_slice_in_dim(strip, section, 3, 0)
    output = convolve(half.reshape(1), frames, next_pair(frames, SP), kernel, bias[None])
    return output.reshape(1, 1, 2, 40, kernel.shape[1])


def solution(mesh):
    fine = Mesh(mesh.devices.reshape(4, 4, 4, 8), ("sec", *SP))
    placed = (
        P(SP, "sec"),
        P(SP, "sec"),
        P(SP, "sec"),
        P(None, SP),
        P(None, SP),
        P("sec", None),
        P(),
        P(),
        P(None, SP, None, None, None),
    )
    return jax.shard_map(
        on_device,
        mesh=fine,
        in_specs=placed,
        out_specs=P("sec", SP, None, None, None),
        check_vma=False,
    )
```

profile of v0, /device:TPU:7, one launch (start us, length us, event | category | flops | bytes accessed | tf_op | source)
XLA Modules:
  0.0 116.3 jit_solution(6203871617576386906)
XLA Ops:
  0.0 3.0 %prepare.1 = bf16[8,248,128]{2,1,0:T(8,128)(2,1)} custom-call(s32[3,80]{1,0:T(4,128)} %qpos.1, s32[3,96]{1,0:T(4,128)} %kpos.1, f32[1,128]{1,0:T(1,128)} %constant.64.clone.freq, bf16[2,128,64]{2,1,0:T(8,128)(2,1)} %constant.65.clone.order, bf16[2,24,40]{2,1,0:T(8,128)(2,1)} %constant.66.clone.pick, bf16[2,64,128]{2,1,0:T(8,128)(2,1)} %constant.67.clone.place, ...), custom_call_target="tpu_custom_call" | custom-call | flops 50000000 | bytes 1200000 | tf_op jit(solution)/shard_map/prepare/pallas_call | solution.py:137
  3.0 22.5 %all_to_all.25.own = bf16[8,248,128]{2,1,0:T(8,128)(2,1)S(1)} all-to-all(bf16[8,248,128]{2,1,0:T(8,128)(2,1)} %prepare.1), channel_id=1, replica_groups=mesh['sec'=4,'x'=4,'zh'=4,'y'=8] {'y'}, dimensions={0} | all-to-all | bytes 1015808 | tf_op jit(solution)/shard_map/all_to_all | solution.py:425
  25.5 0.9 spread.1
  26.5 10.0 %all-to-all-start.1 = ((bf16[4,8,80,128]{3,2,1,0:T(8,128)(2,1)}), bf16[4,8,80,128]{3,2,1,0:T(8,128)(2,1)S(1)}, u32[]{:S(2)}, u32[]{:S(2)}) async-start(bf16[4,8,80,128]{3,2,1,0:T(8,128)(2,1)} %get-tuple-element.15), calls=%async_computation.1 | async-start | bytes 1310720 | tf_op jit(solution)/shard_map/all_to_all | solution.py:427
  36.5 2.1 %collective-permute-start.1 = (bf16[8,144,128]{2,1,0:T(8,128)(2,1)S(1)}, bf16[8,144,128]{2,1,0:T(8,128)(2,1)S(1)}, u32[]{:S(2)}, u32[]{:S(2)}) collective-permute-start(bf16[8,144,128]{2,1,0:T(8,128)(2,1)S(1)} %get-tuple-element.20.refs_1_), channel_id=1, source_target_pairs={{96,0},{0,32},{32,64},{64,96},{97,1},{1,33},{33,65},{65,97},{98,2}... | collective-permute-start | bytes 884744 | tf_op jit(solution)/shard_map/ppermute | solution.py:404
  38.6 3.2 %collective-permute-start = (bf16[8,144,128]{2,1,0:T(8,128)(2,1)S(1)}, bf16[8,144,128]{2,1,0:T(8,128)(2,1)S(1)}, u32[]{:S(2)}, u32[]{:S(2)}) collective-permute-start(bf16[8,144,128]{2,1,0:T(8,128)(2,1)S(1)} %get-tuple-element.20.refs_1_), channel_id=1, source_target_pairs={{32,0},{64,32},{96,64},{0,96},{33,1},{65,33},{97,65},{1,97},{34,2}... | collective-permute-start | bytes 884744 | tf_op jit(solution)/shard_map/ppermute | solution.py:404
  41.8 3.0 %collective-permute-start.2 = (bf16[4,144,128]{2,1,0:T(8,128)(2,1)S(1)}, bf16[4,144,128]{2,1,0:T(8,128)(2,1)S(1)}, u32[]{:S(2)}, u32[]{:S(2)}) collective-permute-start(bf16[4,144,128]{2,1,0:T(8,128)(2,1)S(1)} %slice.9), channel_id=1, source_target_pairs={{64,0},{96,32},{0,64},{32,96},{65,1},{97,33},{1,65},{33,97},{66,2}... | collective-permute-start | bytes 442376 | tf_op jit(solution)/shard_map/ppermute | solution.py:404
  44.8 0.0 collective-permute-done.1.refs_3_
  44.9 3.7 %collective-permute-start.3 = (bf16[4,144,128]{2,1,0:T(8,128)(2,1)S(1)}, bf16[4,144,128]{2,1,0:T(8,128)(2,1)S(1)}, u32[]{:S(2)}, u32[]{:S(2)}) collective-permute-start(bf16[4,144,128]{2,1,0:T(8,128)(2,1)S(1)} %slice.12), channel_id=1, source_target_pairs={{96,0},{0,32},{32,64},{64,96},{97,1},{1,33},{33,65},{65,97},{98,2}... | collective-permute-start | bytes 442376 | tf_op jit(solution)/shard_map/ppermute | solution.py:404
  48.7 0.1 reshape.34
  48.8 0.1 reshape.35
  48.9 2.0 %collective-permute-done.2.refs_4_ = bf16[4,144,128]{2,1,0:T(8,128)(2,1)S(1)} collective-permute-done((bf16[4,144,128]{2,1,0:T(8,128)(2,1)S(1)}, bf16[4,144,128]{2,1,0:T(8,128)(2,1)S(1)}, u32[]{:S(2)}, u32[]{:S(2)}) %collective-permute-start.2) | collective-permute-done | bytes 147488 | tf_op jit(solution)/shard_map/ppermute | solution.py:404
  51.0 0.0 collective-permute-done.refs_2_
  51.0 1.3 %collective-permute-done.3.refs_5_ = bf16[4,144,128]{2,1,0:T(8,128)(2,1)S(1)} collective-permute-done((bf16[4,144,128]{2,1,0:T(8,128)(2,1)S(1)}, bf16[4,144,128]{2,1,0:T(8,128)(2,1)S(1)}, u32[]{:S(2)}, u32[]{:S(2)}) %collective-permute-start.3) | collective-permute-done | bytes 147488 | tf_op jit(solution)/shard_map/ppermute | solution.py:404
  52.3 0.0 all-to-all-done.1
  52.3 9.3 %attend.1 = bf16[4,352,128]{2,1,0:T(8,128)(2,1)S(1)} custom-call(bf16[2560,128]{1,0:T(8,128)(2,1)S(1)} %bitcast.13, bf16[8,144,128]{2,1,0:T(8,128)(2,1)S(1)} %get-tuple-element.20.refs_1_, bf16[8,144,128]{2,1,0:T(8,128)(2,1)S(1)} %collective-permute-done.refs_2_, bf16[8,144,128]{2,1,0:T(8,128)(2,1)S(1)} %collective-permute-done.1.refs_3_, ...), custom_call_target="tpu_custom_call" | custom-call | flops 4026531840 | bytes 2000000 | tf_op jit(solution)/shard_map/attend/pallas_call | solution.py:271
  61.6 16.6 %all_to_all.26.r_ref = bf16[4,352,128]{2,1,0:T(8,128)(2,1)S(1)} all-to-all(bf16[4,352,128]{2,1,0:T(8,128)(2,1)S(1)} %attend.1), channel_id=1, replica_groups=mesh['sec'=4,'x'=4,'zh'=4,'y'=8] {'zh'}, dimensions={0} | all-to-all | bytes 720896 | tf_op jit(solution)/shard_map/all_to_all | solution.py:433
  78.2 1.3 %combine.1 = bf16[8,4,24,128]{3,2,1,0:T(8,128)(2,1)S(1)} custom-call(bf16[4,352,128]{2,1,0:T(8,128)(2,1)S(1)} %all_to_all.26.r_ref), custom_call_target="tpu_custom_call" | custom-call | flops 1000000 | bytes 900000 | tf_op jit(solution)/shard_map/combine/pallas_call | solution.py:330
  79.4 11.3 %all_to_all.27.parts = bf16[8,4,24,128]{3,2,1,0:T(8,128)(2,1)S(1)} all-to-all(bf16[8,4,24,128]{3,2,1,0:T(8,128)(2,1)S(1)} %combine.1), channel_id=1, replica_groups=mesh['sec'=4,'x'=4,'zh'=4,'y'=8] {'y'}, dimensions={0} | all-to-all | bytes 393216 | tf_op jit(solution)/shard_map/all_to_all | solution.py:434
  90.7 0.0 copy-start
  90.7 0.7 add_heads.1
  91.4 12.0 %all-to-all-start.4 = ((bf16[16,24,128]{2,1,0:T(8,128)(2,1)}), bf16[16,24,128]{2,1,0:T(8,128)(2,1)S(1)}, u32[]{:S(2)}, u32[]{:S(2)}) async-start(bf16[16,24,128]{2,1,0:T(8,128)(2,1)} %bitcast.8), calls=%async_computation.4 | async-start | bytes 196608 | tf_op jit(solution)/shard_map/all_to_all | solution.py:435
  103.4 4.2 %all-to-all-done.4 = bf16[16,24,128]{2,1,0:T(8,128)(2,1)S(1)} async-done(((bf16[16,24,128]{2,1,0:T(8,128)(2,1)}), bf16[16,24,128]{2,1,0:T(8,128)(2,1)S(1)}, u32[]{:S(2)}, u32[]{:S(2)}) %all-to-all-start.4) | async-done | bytes 98336 | tf_op jit(solution)/shard_map/all_to_all | solution.py:435
  107.7 1.9 %collective-permute-start.4 = (bf16[3,24,128]{2,1,0:T(8,128)(2,1)S(1)}, bf16[3,24,128]{2,1,0:T(8,128)(2,1)S(1)}, u32[]{:S(2)}, u32[]{:S(2)}) collective-permute-start(bf16[3,24,128]{2,1,0:T(8,128)(2,1)S(1)} %fusion.own), channel_id=1, source_target_pairs={{0,8},{1,9},{2,10},{3,11},{8,16},{9,17},{10,18},{11,19},{16,24},{1... | collective-permute-start | bytes 55304 | tf_op jit(solution)/shard_map/ppermute | solution.py:409
  109.7 0.0 copy-start.1
  109.7 0.7 copy-done.1
  110.3 4.9 %collective-permute-done.4.near = bf16[3,24,128]{2,1,0:T(8,128)(2,1)S(1)} collective-permute-done((bf16[3,24,128]{2,1,0:T(8,128)(2,1)S(1)}, bf16[3,24,128]{2,1,0:T(8,128)(2,1)S(1)}, u32[]{:S(2)}, u32[]{:S(2)}) %collective-permute-start.4) | collective-permute-done | bytes 18464 | tf_op jit(solution)/shard_map/ppermute | solution.py:409
  115.2 0.0 copy-done
  115.2 1.1 convolve.1
  (9 shorter events, 0.2 us)
Async XLA Ops:
  26.5 25.8 %all-to-all-start.1 = ((bf16[4,8,80,128]{3,2,1,0:T(8,128)(2,1)}), bf16[4,8,80,128]{3,2,1,0:T(8,128)(2,1)S(1)}, u32[]{:S(2)}, u32[]{:S(2)}) async-start(bf16[4,8,80,128]{3,2,1,0:T(8,128)(2,1)} %get-tuple-element.15), calls=%async_computation.1 | async-start | bytes 1310720 | tf_op jit(solution)/shard_map/all_to_all | solution.py:427
  36.5 8.3 %collective-permute-start.1 = (bf16[8,144,128]{2,1,0:T(8,128)(2,1)S(1)}, bf16[8,144,128]{2,1,0:T(8,128)(2,1)S(1)}, u32[]{:S(2)}, u32[]{:S(2)}) collective-permute-start(bf16[8,144,128]{2,1,0:T(8,128)(2,1)S(1)} %get-tuple-element.20.refs_1_), channel_id=1, source_target_pairs={{96,0},{0,32},{32,64},{64,96},{97,1},{1,33},{33,65},{65,97},{98,2}... | collective-permute-start | bytes 884744 | tf_op jit(solution)/shard_map/ppermute | solution.py:404
  38.6 12.4 %collective-permute-start = (bf16[8,144,128]{2,1,0:T(8,128)(2,1)S(1)}, bf16[8,144,128]{2,1,0:T(8,128)(2,1)S(1)}, u32[]{:S(2)}, u32[]{:S(2)}) collective-permute-start(bf16[8,144,128]{2,1,0:T(8,128)(2,1)S(1)} %get-tuple-element.20.refs_1_), channel_id=1, source_target_pairs={{32,0},{64,32},{96,64},{0,96},{33,1},{65,33},{97,65},{1,97},{34,2}... | collective-permute-start | bytes 884744 | tf_op jit(solution)/shard_map/ppermute | solution.py:404
  41.8 9.2 %collective-permute-start.2 = (bf16[4,144,128]{2,1,0:T(8,128)(2,1)S(1)}, bf16[4,144,128]{2,1,0:T(8,128)(2,1)S(1)}, u32[]{:S(2)}, u32[]{:S(2)}) collective-permute-start(bf16[4,144,128]{2,1,0:T(8,128)(2,1)S(1)} %slice.9), channel_id=1, source_target_pairs={{64,0},{96,32},{0,64},{32,96},{65,1},{97,33},{1,65},{33,97},{66,2}... | collective-permute-start | bytes 442376 | tf_op jit(solution)/shard_map/ppermute | solution.py:404
  44.9 7.4 %collective-permute-start.3 = (bf16[4,144,128]{2,1,0:T(8,128)(2,1)S(1)}, bf16[4,144,128]{2,1,0:T(8,128)(2,1)S(1)}, u32[]{:S(2)}, u32[]{:S(2)}) collective-permute-start(bf16[4,144,128]{2,1,0:T(8,128)(2,1)S(1)} %slice.12), channel_id=1, source_target_pairs={{96,0},{0,32},{32,64},{64,96},{97,1},{1,33},{33,65},{65,97},{98,2}... | collective-permute-start | bytes 442376 | tf_op jit(solution)/shard_map/ppermute | solution.py:404
  90.7 24.5 %copy-start = (bf16[432,384]{1,0:T(8,128)(2,1)S(1)}, bf16[432,384]{1,0:T(8,128)(2,1)}, u32[]{:S(2)}) copy-start(bf16[432,384]{1,0:T(8,128)(2,1)} %kernel.1) | copy-start | bytes 995332
  91.4 16.2 %all-to-all-start.4 = ((bf16[16,24,128]{2,1,0:T(8,128)(2,1)}), bf16[16,24,128]{2,1,0:T(8,128)(2,1)S(1)}, u32[]{:S(2)}, u32[]{:S(2)}) async-start(bf16[16,24,128]{2,1,0:T(8,128)(2,1)} %bitcast.8), calls=%async_computation.4 | async-start | bytes 196608 | tf_op jit(solution)/shard_map/all_to_all | solution.py:435
  107.7 7.5 %collective-permute-start.4 = (bf16[3,24,128]{2,1,0:T(8,128)(2,1)S(1)}, bf16[3,24,128]{2,1,0:T(8,128)(2,1)S(1)}, u32[]{:S(2)}, u32[]{:S(2)}) collective-permute-start(bf16[3,24,128]{2,1,0:T(8,128)(2,1)S(1)} %fusion.own), channel_id=1, source_target_pairs={{0,8},{1,9},{2,10},{3,11},{8,16},{9,17},{10,18},{11,19},{16,24},{1... | collective-permute-start | bytes 55304 | tf_op jit(solution)/shard_map/ppermute | solution.py:409
  109.7 0.7 copy-start.1
where the time goes:
time: 118 us; the launch traced here: 116 us
  blocking collectives  50.4 us (43%)
  starting transfers between devices  36 us (31%)
  Pallas kernels  16.3 us (14%)
  waiting for transfers between devices  12.5 us (11%)
    all_to_all x1, blocking collectives, on_device(): own = lax.all_to_all(own, 'y', 0, 0)  22.5 us
    all_to_all x1, blocking collectives, on_device(): shares = lax.all_to_all(parts, 'zh', 0, 0)  16.6 us
    ppermute x4, starting transfers between devices, from_ahead(): lax.ppermute(value, axis, [((spot + steps) % 4, spot) for spot in range(4)])  12 us
    all_to_all x1, starting transfers between devices, on_device(): lax.all_to_all(add_heads(tiles).reshape(16, STRIP, HD), ('sec', 'x'), 0, 0)  12 us
    all_to_all x1, blocking collectives, on_device(): tiles = lax.all_to_all(combine(shares), 'y', 0, 0)  11.3 us
    all_to_all x1, starting transfers between devices, on_device(): query_all = lax.all_to_all(q_copies, 'zh', 0, 0)  10 us
    pallas_call x1, Pallas kernels, attend(): pl.pallas_call(attend_kernel, in_specs=[HERE] * 6, out_specs=HERE, out_sh...  9.34 us
    ppermute x1, waiting for transfers between devices, next_pair(): return lax.ppermute(value, axes, pairs)  4.89 us
  transfers between devices with their start and end apart: 7, of which 4 were waited for; matrix products, arithmetic and copies ran while one was open for 0% of the time, Pallas kernels for 0%

commit v1 on v0

--- a/solution.py
+++ b/solution.py
@@ -16,7 +16,8 @@
 K_OWN = 96
 V_ROWS = K_OWN // 2
 KV_ROWS = K_OWN + V_ROWS
-OWN_ROWS = KV_ROWS + Q_OWN + STRIP
+TILE_ROWS = 32
+OWN_ROWS = KV_ROWS + Q_OWN + TILE_ROWS
 MIX = 64
 GRID_W = 80
 HALF_W = GRID_W // 2
@@ -52,7 +53,7 @@
 
 
 def patch_order():
-    pick = np.zeros((2, STRIP, 40), np.float32)
+    pick = np.zeros((2, TILE_ROWS, 40), np.float32)
     place = np.zeros((2, MIX, HD), np.float32)
     for side in range(2):
         for patch in range(TILE_W):
@@ -107,7 +108,7 @@
 def prepare_kernel(qpos, kpos, freq, order, pick, place, queries, keys, values, mixing, cache, out):
     q_tables = turn_tables(qpos[...], freq[...])
     k_tables = turn_tables(kpos[...], freq[...])
-    tile = jnp.zeros((STRIP, HD), jnp.float32)
+    tile = jnp.zeros((TILE_ROWS, HD), jnp.float32)
     for side in range(2):
         column = lax.dot_general(
             pick[side], cache[...], (((1,), (1,)), ((), ())), preferred_element_type=jnp.float32
@@ -173,7 +174,7 @@
         out_shape=[
             jax.ShapeDtypeStruct((4, HEADS_SEC, Q_OWN, HD), jnp.bfloat16),
             jax.ShapeDtypeStruct((HEADS_SEC, KV_ROWS, HD), jnp.bfloat16),
-            jax.ShapeDtypeStruct((HEADS_SEC, STRIP, HD), jnp.bfloat16),
+            jax.ShapeDtypeStruct((HEADS_SEC, TILE_ROWS, HD), jnp.bfloat16),
         ],
         compiler_params=pltpu.CompilerParams(vmem_limit_bytes=4 * MIB),
         cost_estimate=pl.CostEstimate(flops=0, bytes_accessed=800000, transcendentals=0),
@@ -182,10 +183,10 @@
 
 
 def add_heads_kernel(parts, out):
-    total = parts[0].astype(jnp.float32)
-    for part in range(1, 8):
-        total = total + parts[part].astype(jnp.float32)
-    total = total.astype(jnp.bfloat16)
+    terms = [parts[part].astype(jnp.float32) for part in range(8)]
+    while len(terms) > 1:
+        terms = [terms[i] + terms[i + 1] for i in range(0, len(terms), 2)]
+    total = terms[0].astype(jnp.bfloat16)
     for copy in range(4):
         out[copy] = total
 
@@ -410,7 +411,7 @@
 
 
 def cache_strips(tiles, tile_col):
-    wide = tiles.reshape(2, 4, STRIP, HD)[:, :, :TILE_W].reshape(2, GRID_W, HD)
+    wide = tiles.reshape(2, 4, TILE_ROWS, HD)[:, :, :TILE_W].reshape(2, GRID_W, HD)
     wide = jnp.pad(wide, ((0, 0), (1, 3), (0, 0)))
     wide = lax.dynamic_slice_in_dim(wide, tile_col * TILE_W, STRIP, 1)
     return wide.reshape(2, STRIP, 2, MIX).transpose(2, 1, 0, 3).reshape(2, STRIP, HD)

time: 118 us -> 119 us (level)
  no operation moved by 1% of the time
where the time goes in v1:
time: 119 us; the launch traced here: 117 us
  blocking collectives  50.7 us (43%)
  starting transfers between devices  36 us (30%)
  Pallas kernels  16.2 us (14%)
  waiting for transfers between devices  12.4 us (10%)
    all_to_all x1, blocking collectives, on_device(): own = lax.all_to_all(own, 'y', 0, 0)  22.8 us
    all_to_all x1, blocking collectives, on_device(): shares = lax.all_to_all(parts, 'zh', 0, 0)  16.6 us
    ppermute x4, starting transfers between devices, from_ahead(): lax.ppermute(value, axis, [((spot + steps) % 4, spot) for spot in range(4)])  12 us
    all_to_all x1, starting transfers between devices, on_device(): lax.all_to_all(add_heads(tiles).reshape(16, STRIP, HD), ('sec', 'x'), 0, 0)  12 us
    all_to_all x1, blocking collectives, on_device(): tiles = lax.all_to_all(combine(shares), 'y', 0, 0)  11.4 us
    all_to_all x1, starting transfers between devices, on_device(): query_all = lax.all_to_all(q_copies, 'zh', 0, 0)  10 us
    pallas_call x1, Pallas kernels, attend(): pl.pallas_call(attend_kernel, in_specs=[HERE] * 6, out_specs=HERE, out_sh...  9.34 us
    ppermute x1, waiting for transfers between devices, next_pair(): return lax.ppermute(value, axes, pairs)  4.89 us
  transfers between devices with their start and end apart: 7, of which 4 were waited for; matrix products, arithmetic and copies ran while one was open for 0% of the time, Pallas kernels for 0%

profile of v1, /device:TPU:7, one launch (start us, length us, event | category | flops | bytes accessed | tf_op | source)
XLA Modules:
  0.0 116.6 jit_solution(14803111498401197649)
XLA Ops:
  0.0 3.0 %prepare.1 = bf16[8,256,128]{2,1,0:T(8,128)(2,1)} custom-call(s32[3,80]{1,0:T(4,128)} %qpos.1, s32[3,96]{1,0:T(4,128)} %kpos.1, f32[1,128]{1,0:T(1,128)} %constant.64.clone.freq, bf16[2,128,64]{2,1,0:T(8,128)(2,1)} %constant.65.clone.order, bf16[2,32,40]{2,1,0:T(8,128)(2,1)} %constant.66.clone.pick, bf16[2,64,128]{2,1,0:T(8,128)(2,1)} %constant.67.clone.place, ...), custom_call_target="tpu_custom_call" | custom-call | flops 50000000 | bytes 1200000 | tf_op jit(solution)/shard_map/prepare/pallas_call | solution.py:138
  3.0 22.8 %all_to_all.25.own = bf16[8,256,128]{2,1,0:T(8,128)(2,1)S(1)} all-to-all(bf16[8,256,128]{2,1,0:T(8,128)(2,1)} %prepare.1), channel_id=1, replica_groups=mesh['sec'=4,'x'=4,'zh'=4,'y'=8] {'y'}, dimensions={0} | all-to-all | bytes 1048576 | tf_op jit(solution)/shard_map/all_to_all | solution.py:426
  25.8 0.9 spread.1
  26.7 10.0 %all-to-all-start.1 = ((bf16[4,8,80,128]{3,2,1,0:T(8,128)(2,1)}), bf16[4,8,80,128]{3,2,1,0:T(8,128)(2,1)S(1)}, u32[]{:S(2)}, u32[]{:S(2)}) async-start(bf16[4,8,80,128]{3,2,1,0:T(8,128)(2,1)} %get-tuple-element.15), calls=%async_computation.1 | async-start | bytes 1310720 | tf_op jit(solution)/shard_map/all_to_all | solution.py:428
  36.7 2.1 %collective-permute-start.1 = (bf16[8,144,128]{2,1,0:T(8,128)(2,1)S(1)}, bf16[8,144,128]{2,1,0:T(8,128)(2,1)S(1)}, u32[]{:S(2)}, u32[]{:S(2)}) collective-permute-start(bf16[8,144,128]{2,1,0:T(8,128)(2,1)S(1)} %get-tuple-element.20.refs_1_), channel_id=1, source_target_pairs={{96,0},{0,32},{32,64},{64,96},{97,1},{1,33},{33,65},{65,97},{98,2}... | collective-permute-start | bytes 884744 | tf_op jit(solution)/shard_map/ppermute | solution.py:405
  38.8 3.2 %collective-permute-start = (bf16[8,144,128]{2,1,0:T(8,128)(2,1)S(1)}, bf16[8,144,128]{2,1,0:T(8,128)(2,1)S(1)}, u32[]{:S(2)}, u32[]{:S(2)}) collective-permute-start(bf16[8,144,128]{2,1,0:T(8,128)(2,1)S(1)} %get-tuple-element.20.refs_1_), channel_id=1, source_target_pairs={{32,0},{64,32},{96,64},{0,96},{33,1},{65,33},{97,65},{1,97},{34,2}... | collective-permute-start | bytes 884744 | tf_op jit(solution)/shard_map/ppermute | solution.py:405
  42.0 3.0 %collective-permute-start.2 = (bf16[4,144,128]{2,1,0:T(8,128)(2,1)S(1)}, bf16[4,144,128]{2,1,0:T(8,128)(2,1)S(1)}, u32[]{:S(2)}, u32[]{:S(2)}) collective-permute-start(bf16[4,144,128]{2,1,0:T(8,128)(2,1)S(1)} %slice.9), channel_id=1, source_target_pairs={{64,0},{96,32},{0,64},{32,96},{65,1},{97,33},{1,65},{33,97},{66,2}... | collective-permute-start | bytes 442376 | tf_op jit(solution)/shard_map/ppermute | solution.py:405
  45.1 0.0 collective-permute-done.1.refs_3_
  45.1 3.7 %collective-permute-start.3 = (bf16[4,144,128]{2,1,0:T(8,128)(2,1)S(1)}, bf16[4,144,128]{2,1,0:T(8,128)(2,1)S(1)}, u32[]{:S(2)}, u32[]{:S(2)}) collective-permute-start(bf16[4,144,128]{2,1,0:T(8,128)(2,1)S(1)} %slice.12), channel_id=1, source_target_pairs={{96,0},{0,32},{32,64},{64,96},{97,1},{1,33},{33,65},{65,97},{98,2}... | collective-permute-start | bytes 442376 | tf_op jit(solution)/shard_map/ppermute | solution.py:405
  49.0 0.1 reshape.34
  49.1 0.1 reshape.35
  49.2 2.1 %collective-permute-done.2.refs_4_ = bf16[4,144,128]{2,1,0:T(8,128)(2,1)S(1)} collective-permute-done((bf16[4,144,128]{2,1,0:T(8,128)(2,1)S(1)}, bf16[4,144,128]{2,1,0:T(8,128)(2,1)S(1)}, u32[]{:S(2)}, u32[]{:S(2)}) %collective-permute-start.2) | collective-permute-done | bytes 147488 | tf_op jit(solution)/shard_map/ppermute | solution.py:405
  51.3 0.0 collective-permute-done.refs_2_
  51.3 1.2 %collective-permute-done.3.refs_5_ = bf16[4,144,128]{2,1,0:T(8,128)(2,1)S(1)} collective-permute-done((bf16[4,144,128]{2,1,0:T(8,128)(2,1)S(1)}, bf16[4,144,128]{2,1,0:T(8,128)(2,1)S(1)}, u32[]{:S(2)}, u32[]{:S(2)}) %collective-permute-start.3) | collective-permute-done | bytes 147488 | tf_op jit(solution)/shard_map/ppermute | solution.py:405
  52.5 0.0 all-to-all-done.1
  52.5 9.3 %attend.1 = bf16[4,352,128]{2,1,0:T(8,128)(2,1)S(1)} custom-call(bf16[2560,128]{1,0:T(8,128)(2,1)S(1)} %bitcast.12, bf16[8,144,128]{2,1,0:T(8,128)(2,1)S(1)} %get-tuple-element.20.refs_1_, bf16[8,144,128]{2,1,0:T(8,128)(2,1)S(1)} %collective-permute-done.refs_2_, bf16[8,144,128]{2,1,0:T(8,128)(2,1)S(1)} %collective-permute-done.1.refs_3_, ...), custom_call_target="tpu_custom_call" | custom-call | flops 4026531840 | bytes 2000000 | tf_op jit(solution)/shard_map/attend/pallas_call | solution.py:272
  61.8 16.6 %all_to_all.26.r_ref = bf16[4,352,128]{2,1,0:T(8,128)(2,1)S(1)} all-to-all(bf16[4,352,128]{2,1,0:T(8,128)(2,1)S(1)} %attend.1), channel_id=1, replica_groups=mesh['sec'=4,'x'=4,'zh'=4,'y'=8] {'zh'}, dimensions={0} | all-to-all | bytes 720896 | tf_op jit(solution)/shard_map/all_to_all | solution.py:434
  78.4 1.3 %combine.1 = bf16[8,4,24,128]{3,2,1,0:T(8,128)(2,1)S(1)} custom-call(bf16[4,352,128]{2,1,0:T(8,128)(2,1)S(1)} %all_to_all.26.r_ref), custom_call_target="tpu_custom_call" | custom-call | flops 1000000 | bytes 900000 | tf_op jit(solution)/shard_map/combine/pallas_call | solution.py:331
  79.7 11.4 %all_to_all.27.parts = bf16[8,4,24,128]{3,2,1,0:T(8,128)(2,1)S(1)} all-to-all(bf16[8,4,24,128]{3,2,1,0:T(8,128)(2,1)S(1)} %combine.1), channel_id=1, replica_groups=mesh['sec'=4,'x'=4,'zh'=4,'y'=8] {'y'}, dimensions={0} | all-to-all | bytes 393216 | tf_op jit(solution)/shard_map/all_to_all | solution.py:435
  91.0 0.0 copy-start
  91.0 0.7 add_heads.1
  91.7 12.0 %all-to-all-start.4 = ((bf16[16,24,128]{2,1,0:T(8,128)(2,1)}), bf16[16,24,128]{2,1,0:T(8,128)(2,1)S(1)}, u32[]{:S(2)}, u32[]{:S(2)}) async-start(bf16[16,24,128]{2,1,0:T(8,128)(2,1)} %bitcast.8), calls=%async_computation.4 | async-start | bytes 196608 | tf_op jit(solution)/shard_map/all_to_all | solution.py:436
  103.7 4.2 %all-to-all-done.4 = bf16[16,24,128]{2,1,0:T(8,128)(2,1)S(1)} async-done(((bf16[16,24,128]{2,1,0:T(8,128)(2,1)}), bf16[16,24,128]{2,1,0:T(8,128)(2,1)S(1)}, u32[]{:S(2)}, u32[]{:S(2)}) %all-to-all-start.4) | async-done | bytes 98336 | tf_op jit(solution)/shard_map/all_to_all | solution.py:436
  108.0 1.9 %collective-permute-start.4 = (bf16[3,24,128]{2,1,0:T(8,128)(2,1)S(1)}, bf16[3,24,128]{2,1,0:T(8,128)(2,1)S(1)}, u32[]{:S(2)}, u32[]{:S(2)}) collective-permute-start(bf16[3,24,128]{2,1,0:T(8,128)(2,1)S(1)} %fusion.own), channel_id=1, source_target_pairs={{0,8},{1,9},{2,10},{3,11},{8,16},{9,17},{10,18},{11,19},{16,24},{1... | collective-permute-start | bytes 55304 | tf_op jit(solution)/shard_map/ppermute | solution.py:410
  109.9 0.0 copy-start.1
  109.9 0.7 copy-done.1
  110.6 4.9 %collective-permute-done.4.near = bf16[3,24,128]{2,1,0:T(8,128)(2,1)S(1)} collective-permute-done((bf16[3,24,128]{2,1,0:T(8,128)(2,1)S(1)}, bf16[3,24,128]{2,1,0:T(8,128)(2,1)S(1)}, u32[]{:S(2)}, u32[]{:S(2)}) %collective-permute-start.4) | collective-permute-done | bytes 18464 | tf_op jit(solution)/shard_map/ppermute | solution.py:410
  115.5 0.0 copy-done
  115.5 1.1 convolve.1
  (10 shorter events, 0.2 us)
Async XLA Ops:
  26.7 25.8 %all-to-all-start.1 = ((bf16[4,8,80,128]{3,2,1,0:T(8,128)(2,1)}), bf16[4,8,80,128]{3,2,1,0:T(8,128)(2,1)S(1)}, u32[]{:S(2)}, u32[]{:S(2)}) async-start(bf16[4,8,80,128]{3,2,1,0:T(8,128)(2,1)} %get-tuple-element.15), calls=%async_computation.1 | async-start | bytes 1310720 | tf_op jit(solution)/shard_map/all_to_all | solution.py:428
  36.7 8.3 %collective-permute-start.1 = (bf16[8,144,128]{2,1,0:T(8,128)(2,1)S(1)}, bf16[8,144,128]{2,1,0:T(8,128)(2,1)S(1)}, u32[]{:S(2)}, u32[]{:S(2)}) collective-permute-start(bf16[8,144,128]{2,1,0:T(8,128)(2,1)S(1)} %get-tuple-element.20.refs_1_), channel_id=1, source_target_pairs={{96,0},{0,32},{32,64},{64,96},{97,1},{1,33},{33,65},{65,97},{98,2}... | collective-permute-start | bytes 884744 | tf_op jit(solution)/shard_map/ppermute | solution.py:405
  38.8 12.5 %collective-permute-start = (bf16[8,144,128]{2,1,0:T(8,128)(2,1)S(1)}, bf16[8,144,128]{2,1,0:T(8,128)(2,1)S(1)}, u32[]{:S(2)}, u32[]{:S(2)}) collective-permute-start(bf16[8,144,128]{2,1,0:T(8,128)(2,1)S(1)} %get-tuple-element.20.refs_1_), channel_id=1, source_target_pairs={{32,0},{64,32},{96,64},{0,96},{33,1},{65,33},{97,65},{1,97},{34,2}... | collective-permute-start | bytes 884744 | tf_op jit(solution)/shard_map/ppermute | solution.py:405
  42.0 9.3 %collective-permute-start.2 = (bf16[4,144,128]{2,1,0:T(8,128)(2,1)S(1)}, bf16[4,144,128]{2,1,0:T(8,128)(2,1)S(1)}, u32[]{:S(2)}, u32[]{:S(2)}) collective-permute-start(bf16[4,144,128]{2,1,0:T(8,128)(2,1)S(1)} %slice.9), channel_id=1, source_target_pairs={{64,0},{96,32},{0,64},{32,96},{65,1},{97,33},{1,65},{33,97},{66,2}... | collective-permute-start | bytes 442376 | tf_op jit(solution)/shard_map/ppermute | solution.py:405
  45.1 7.4 %collective-permute-start.3 = (bf16[4,144,128]{2,1,0:T(8,128)(2,1)S(1)}, bf16[4,144,128]{2,1,0:T(8,128)(2,1)S(1)}, u32[]{:S(2)}, u32[]{:S(2)}) collective-permute-start(bf16[4,144,128]{2,1,0:T(8,128)(2,1)S(1)} %slice.12), channel_id=1, source_target_pairs={{96,0},{0,32},{32,64},{64,96},{97,1},{1,33},{33,65},{65,97},{98,2}... | collective-permute-start | bytes 442376 | tf_op jit(solution)/shard_map/ppermute | solution.py:405
  91.0 24.5 %copy-start = (bf16[432,384]{1,0:T(8,128)(2,1)S(1)}, bf16[432,384]{1,0:T(8,128)(2,1)}, u32[]{:S(2)}) copy-start(bf16[432,384]{1,0:T(8,128)(2,1)} %kernel.1) | copy-start | bytes 995332
  91.7 16.2 %all-to-all-start.4 = ((bf16[16,24,128]{2,1,0:T(8,128)(2,1)}), bf16[16,24,128]{2,1,0:T(8,128)(2,1)S(1)}, u32[]{:S(2)}, u32[]{:S(2)}) async-start(bf16[16,24,128]{2,1,0:T(8,128)(2,1)} %bitcast.8), calls=%async_computation.4 | async-start | bytes 196608 | tf_op jit(solution)/shard_map/all_to_all | solution.py:436
  108.0 7.5 %collective-permute-start.4 = (bf16[3,24,128]{2,1,0:T(8,128)(2,1)S(1)}, bf16[3,24,128]{2,1,0:T(8,128)(2,1)S(1)}, u32[]{:S(2)}, u32[]{:S(2)}) collective-permute-start(bf16[3,24,128]{2,1,0:T(8,128)(2,1)S(1)} %fusion.own), channel_id=1, source_target_pairs={{0,8},{1,9},{2,10},{3,11},{8,16},{9,17},{10,18},{11,19},{16,24},{1... | collective-permute-start | bytes 55304 | tf_op jit(solution)/shard_map/ppermute | solution.py:410
  109.9 0.7 copy-start.1

commit v2 on v1

--- a/solution.py
+++ b/solution.py
@@ -105,9 +105,15 @@
     return out.astype(jnp.bfloat16)
 
 
-def prepare_kernel(qpos, kpos, freq, order, pick, place, queries, keys, values, mixing, cache, out):
-    q_tables = turn_tables(qpos[...], freq[...])
-    k_tables = turn_tables(kpos[...], freq[...])
+def prepare_kernel(qpos, kpos, freq, order, pick, place, queries, keys, values, mixing, cache, out, q_kept, k_kept):
+    @pl.when(pl.program_id(0) == 0)
+    def _():
+        for kept, spots in ((q_kept, qpos), (k_kept, kpos)):
+            for index, table in enumerate(turn_tables(spots[...], freq[...])):
+                kept[index] = table
+
+    q_tables = [q_kept[index] for index in range(3)]
+    k_tables = [k_kept[index] for index in range(3)]
     tile = jnp.zeros((TILE_ROWS, HD), jnp.float32)
     for side in range(2):
         column = lax.dot_general(
@@ -119,7 +125,7 @@
         jnp.dot(order[side], mixing[...], preferred_element_type=jnp.float32).astype(jnp.bfloat16)
         for side in range(2)
     ]
-    for head in range(HEADS_SEC):
+    for head in range(HEADS_SEC // 2):
         cols = slice(head * HD, (head + 1) * HD)
         out[head, 0:K_OWN, :] = turn(keys[:, cols], k_tables)
         value = values[:, cols]
@@ -137,8 +143,22 @@
 def prepare(qpos, kpos, queries, keys, values, mixing, cache):
     return pl.pallas_call(
         prepare_kernel,
-        in_specs=[HERE] * 11,
-        out_specs=HERE,
+        grid=(2,),
+        in_specs=[
+            pl.BlockSpec((3, Q_OWN), lambda i: (0, 0)),
+            pl.BlockSpec((3, K_OWN), lambda i: (0, 0)),
+            pl.BlockSpec((1, HD), lambda i: (0, 0)),
+            pl.BlockSpec((2, HD, MIX), lambda i: (0, 0, 0)),
+            pl.BlockSpec((2, TILE_ROWS, 40), lambda i: (0, 0, 0)),
+            pl.BlockSpec((2, MIX, HD), lambda i: (0, 0, 0)),
+            pl.BlockSpec((Q_OWN, 4 * HD), lambda i: (0, i)),
+            pl.BlockSpec((K_OWN, 4 * HD), lambda i: (0, i)),
+            pl.BlockSpec((K_OWN, 4 * HD), lambda i: (0, i)),
+            pl.BlockSpec((MIX, 4 * HD), lambda i: (0, i)),
+            pl.BlockSpec((MIX, 40), lambda i: (0, 0)),
+        ],
+        out_specs=pl.BlockSpec((HEADS_SEC // 2, OWN_ROWS, HD), lambda i: (i, 0, 0)),
+        scratch_shapes=[pltpu.VMEM((3, Q_OWN, HD), jnp.float32), pltpu.VMEM((3, K_OWN, HD), jnp.float32)],
         out_shape=jax.ShapeDtypeStruct((HEADS_SEC, OWN_ROWS, HD), jnp.bfloat16),
         compiler_params=pltpu.CompilerParams(vmem_limit_bytes=56 * MIB),
         cost_estimate=pl.CostEstimate(flops=50000000, bytes_accessed=1200000, transcendentals=0),

time: 119 us -> 119 us (level)
  no operation moved by 1% of the time
where the time goes in v2:
time: 119 us; the launch traced here: 117 us
  blocking collectives  50.8 us (43%)
  starting transfers between devices  36 us (30%)
  Pallas kernels  16.5 us (14%)
  waiting for transfers between devices  12.4 us (10%)
    all_to_all x1, blocking collectives, on_device(): own = lax.all_to_all(own, 'y', 0, 0)  22.8 us
    all_to_all x1, blocking collectives, on_device(): shares = lax.all_to_all(parts, 'zh', 0, 0)  16.6 us
    ppermute x4, starting transfers between devices, from_ahead(): lax.ppermute(value, axis, [((spot + steps) % 4, spot) for spot in range(4)])  12 us
    all_to_all x1, starting transfers between devices, on_device(): lax.all_to_all(add_heads(tiles).reshape(16, STRIP, HD), ('sec', 'x'), 0, 0)  12 us
    all_to_all x1, blocking collectives, on_device(): tiles = lax.all_to_all(combine(shares), 'y', 0, 0)  11.4 us
    all_to_all x1, starting transfers between devices, on_device(): query_all = lax.all_to_all(q_copies, 'zh', 0, 0)  10 us
    pallas_call x1, Pallas kernels, attend(): pl.pallas_call(attend_kernel, in_specs=[HERE] * 6, out_specs=HERE, out_sh...  9.34 us
    ppermute x1, waiting for transfers between devices, next_pair(): return lax.ppermute(value, axes, pairs)  4.89 us
  transfers between devices with their start and end apart: 7, of which 4 were waited for; matrix products, arithmetic and copies ran while one was open for 0% of the time, Pallas kernels for 0%

profile of v2, /device:TPU:7, one launch (start us, length us, event | category | flops | bytes accessed | tf_op | source)
XLA Modules:
  0.0 116.8 jit_solution(5356702681682853658)
XLA Ops:
  0.0 3.2 %prepare.1 = bf16[8,256,128]{2,1,0:T(8,128)(2,1)} custom-call(s32[3,80]{1,0:T(4,128)} %qpos.1, s32[3,96]{1,0:T(4,128)} %kpos.1, f32[1,128]{1,0:T(1,128)} %constant.64.clone.freq, bf16[2,128,64]{2,1,0:T(8,128)(2,1)} %constant.65.clone.order, bf16[2,32,40]{2,1,0:T(8,128)(2,1)} %constant.66.clone.pick, bf16[2,64,128]{2,1,0:T(8,128)(2,1)} %constant.67.clone.place, ...), custom_call_target="tpu_custom_call" | custom-call | flops 50000000 | bytes 1200000 | tf_op jit(solution)/shard_map/prepare/pallas_call | solution.py:144
  3.2 22.8 %all_to_all.25.own = bf16[8,256,128]{2,1,0:T(8,128)(2,1)S(1)} all-to-all(bf16[8,256,128]{2,1,0:T(8,128)(2,1)} %prepare.1), channel_id=1, replica_groups=mesh['sec'=4,'x'=4,'zh'=4,'y'=8] {'y'}, dimensions={0} | all-to-all | bytes 1048576 | tf_op jit(solution)/shard_map/all_to_all | solution.py:446
  26.1 0.9 spread.1
  27.0 10.0 %all-to-all-start.1 = ((bf16[4,8,80,128]{3,2,1,0:T(8,128)(2,1)}), bf16[4,8,80,128]{3,2,1,0:T(8,128)(2,1)S(1)}, u32[]{:S(2)}, u32[]{:S(2)}) async-start(bf16[4,8,80,128]{3,2,1,0:T(8,128)(2,1)} %get-tuple-element.15), calls=%async_computation.1 | async-start | bytes 1310720 | tf_op jit(solution)/shard_map/all_to_all | solution.py:448
  37.0 2.1 %collective-permute-start.1 = (bf16[8,144,128]{2,1,0:T(8,128)(2,1)S(1)}, bf16[8,144,128]{2,1,0:T(8,128)(2,1)S(1)}, u32[]{:S(2)}, u32[]{:S(2)}) collective-permute-start(bf16[8,144,128]{2,1,0:T(8,128)(2,1)S(1)} %get-tuple-element.20.refs_1_), channel_id=1, source_target_pairs={{96,0},{0,32},{32,64},{64,96},{97,1},{1,33},{33,65},{65,97},{98,2}... | collective-permute-start | bytes 884744 | tf_op jit(solution)/shard_map/ppermute | solution.py:425
  39.1 3.2 %collective-permute-start = (bf16[8,144,128]{2,1,0:T(8,128)(2,1)S(1)}, bf16[8,144,128]{2,1,0:T(8,128)(2,1)S(1)}, u32[]{:S(2)}, u32[]{:S(2)}) collective-permute-start(bf16[8,144,128]{2,1,0:T(8,128)(2,1)S(1)} %get-tuple-element.20.refs_1_), channel_id=1, source_target_pairs={{32,0},{64,32},{96,64},{0,96},{33,1},{65,33},{97,65},{1,97},{34,2}... | collective-permute-start | bytes 884744 | tf_op jit(solution)/shard_map/ppermute | solution.py:425
  42.3 3.0 %collective-permute-start.2 = (bf16[4,144,128]{2,1,0:T(8,128)(2,1)S(1)}, bf16[4,144,128]{2,1,0:T(8,128)(2,1)S(1)}, u32[]{:S(2)}, u32[]{:S(2)}) collective-permute-start(bf16[4,144,128]{2,1,0:T(8,128)(2,1)S(1)} %slice.9), channel_id=1, source_target_pairs={{64,0},{96,32},{0,64},{32,96},{65,1},{97,33},{1,65},{33,97},{66,2}... | collective-permute-start | bytes 442376 | tf_op jit(solution)/shard_map/ppermute | solution.py:425
  45.4 0.0 collective-permute-done.1.refs_3_
  45.4 3.7 %collective-permute-start.3 = (bf16[4,144,128]{2,1,0:T(8,128)(2,1)S(1)}, bf16[4,144,128]{2,1,0:T(8,128)(2,1)S(1)}, u32[]{:S(2)}, u32[]{:S(2)}) collective-permute-start(bf16[4,144,128]{2,1,0:T(8,128)(2,1)S(1)} %slice.12), channel_id=1, source_target_pairs={{96,0},{0,32},{32,64},{64,96},{97,1},{1,33},{33,65},{65,97},{98,2}... | collective-permute-start | bytes 442376 | tf_op jit(solution)/shard_map/ppermute | solution.py:425
  49.3 0.1 reshape.34
  49.4 0.1 reshape.35
  49.5 2.1 %collective-permute-done.2.refs_4_ = bf16[4,144,128]{2,1,0:T(8,128)(2,1)S(1)} collective-permute-done((bf16[4,144,128]{2,1,0:T(8,128)(2,1)S(1)}, bf16[4,144,128]{2,1,0:T(8,128)(2,1)S(1)}, u32[]{:S(2)}, u32[]{:S(2)}) %collective-permute-start.2) | collective-permute-done | bytes 147488 | tf_op jit(solution)/shard_map/ppermute | solution.py:425
  51.6 0.0 collective-permute-done.refs_2_
  51.6 1.2 %collective-permute-done.3.refs_5_ = bf16[4,144,128]{2,1,0:T(8,128)(2,1)S(1)} collective-permute-done((bf16[4,144,128]{2,1,0:T(8,128)(2,1)S(1)}, bf16[4,144,128]{2,1,0:T(8,128)(2,1)S(1)}, u32[]{:S(2)}, u32[]{:S(2)}) %collective-permute-start.3) | collective-permute-done | bytes 147488 | tf_op jit(solution)/shard_map/ppermute | solution.py:425
  52.8 0.0 all-to-all-done.1
  52.8 9.3 %attend.1 = bf16[4,352,128]{2,1,0:T(8,128)(2,1)S(1)} custom-call(bf16[2560,128]{1,0:T(8,128)(2,1)S(1)} %bitcast.12, bf16[8,144,128]{2,1,0:T(8,128)(2,1)S(1)} %get-tuple-element.20.refs_1_, bf16[8,144,128]{2,1,0:T(8,128)(2,1)S(1)} %collective-permute-done.refs_2_, bf16[8,144,128]{2,1,0:T(8,128)(2,1)S(1)} %collective-permute-done.1.refs_3_, ...), custom_call_target="tpu_custom_call" | custom-call | flops 4026531840 | bytes 2000000 | tf_op jit(solution)/shard_map/attend/pallas_call | solution.py:292
  62.1 16.6 %all_to_all.26.r_ref = bf16[4,352,128]{2,1,0:T(8,128)(2,1)S(1)} all-to-all(bf16[4,352,128]{2,1,0:T(8,128)(2,1)S(1)} %attend.1), channel_id=1, replica_groups=mesh['sec'=4,'x'=4,'zh'=4,'y'=8] {'zh'}, dimensions={0} | all-to-all | bytes 720896 | tf_op jit(solution)/shard_map/all_to_all | solution.py:454
  78.7 1.3 %combine.1 = bf16[8,4,24,128]{3,2,1,0:T(8,128)(2,1)S(1)} custom-call(bf16[4,352,128]{2,1,0:T(8,128)(2,1)S(1)} %all_to_all.26.r_ref), custom_call_target="tpu_custom_call" | custom-call | flops 1000000 | bytes 900000 | tf_op jit(solution)/shard_map/combine/pallas_call | solution.py:351
  80.0 11.4 %all_to_all.27.parts = bf16[8,4,24,128]{3,2,1,0:T(8,128)(2,1)S(1)} all-to-all(bf16[8,4,24,128]{3,2,1,0:T(8,128)(2,1)S(1)} %combine.1), channel_id=1, replica_groups=mesh['sec'=4,'x'=4,'zh'=4,'y'=8] {'y'}, dimensions={0} | all-to-all | bytes 393216 | tf_op jit(solution)/shard_map/all_to_all | solution.py:455
  91.3 0.0 copy-start
  91.3 0.7 add_heads.1
  92.0 12.0 %all-to-all-start.4 = ((bf16[16,24,128]{2,1,0:T(8,128)(2,1)}), bf16[16,24,128]{2,1,0:T(8,128)(2,1)S(1)}, u32[]{:S(2)}, u32[]{:S(2)}) async-start(bf16[16,24,128]{2,1,0:T(8,128)(2,1)} %bitcast.8), calls=%async_computation.4 | async-start | bytes 196608 | tf_op jit(solution)/shard_map/all_to_all | solution.py:456
  104.0 4.2 %all-to-all-done.4 = bf16[16,24,128]{2,1,0:T(8,128)(2,1)S(1)} async-done(((bf16[16,24,128]{2,1,0:T(8,128)(2,1)}), bf16[16,24,128]{2,1,0:T(8,128)(2,1)S(1)}, u32[]{:S(2)}, u32[]{:S(2)}) %all-to-all-start.4) | async-done | bytes 98336 | tf_op jit(solution)/shard_map/all_to_all | solution.py:456
  108.3 1.9 %collective-permute-start.4 = (bf16[3,24,128]{2,1,0:T(8,128)(2,1)S(1)}, bf16[3,24,128]{2,1,0:T(8,128)(2,1)S(1)}, u32[]{:S(2)}, u32[]{:S(2)}) collective-permute-start(bf16[3,24,128]{2,1,0:T(8,128)(2,1)S(1)} %fusion.own), channel_id=1, source_target_pairs={{0,8},{1,9},{2,10},{3,11},{8,16},{9,17},{10,18},{11,19},{16,24},{1... | collective-permute-start | bytes 55304 | tf_op jit(solution)/shard_map/ppermute | solution.py:430
  110.2 0.0 copy-start.1
  110.2 0.7 copy-done.1
  110.9 4.9 %collective-permute-done.4.near = bf16[3,24,128]{2,1,0:T(8,128)(2,1)S(1)} collective-permute-done((bf16[3,24,128]{2,1,0:T(8,128)(2,1)S(1)}, bf16[3,24,128]{2,1,0:T(8,128)(2,1)S(1)}, u32[]{:S(2)}, u32[]{:S(2)}) %collective-permute-start.4) | collective-permute-done | bytes 18464 | tf_op jit(solution)/shard_map/ppermute | solution.py:430
  115.8 0.0 copy-done
  115.8 1.1 convolve.1
  (10 shorter events, 0.2 us)
Async XLA Ops:
  27.0 25.8 %all-to-all-start.1 = ((bf16[4,8,80,128]{3,2,1,0:T(8,128)(2,1)}), bf16[4,8,80,128]{3,2,1,0:T(8,128)(2,1)S(1)}, u32[]{:S(2)}, u32[]{:S(2)}) async-start(bf16[4,8,80,128]{3,2,1,0:T(8,128)(2,1)} %get-tuple-element.15), calls=%async_computation.1 | async-start | bytes 1310720 | tf_op jit(solution)/shard_map/all_to_all | solution.py:448
  37.0 8.4 %collective-permute-start.1 = (bf16[8,144,128]{2,1,0:T(8,128)(2,1)S(1)}, bf16[8,144,128]{2,1,0:T(8,128)(2,1)S(1)}, u32[]{:S(2)}, u32[]{:S(2)}) collective-permute-start(bf16[8,144,128]{2,1,0:T(8,128)(2,1)S(1)} %get-tuple-element.20.refs_1_), channel_id=1, source_target_pairs={{96,0},{0,32},{32,64},{64,96},{97,1},{1,33},{33,65},{65,97},{98,2}... | collective-permute-start | bytes 884744 | tf_op jit(solution)/shard_map/ppermute | solution.py:425
  39.1 12.5 %collective-permute-start = (bf16[8,144,128]{2,1,0:T(8,128)(2,1)S(1)}, bf16[8,144,128]{2,1,0:T(8,128)(2,1)S(1)}, u32[]{:S(2)}, u32[]{:S(2)}) collective-permute-start(bf16[8,144,128]{2,1,0:T(8,128)(2,1)S(1)} %get-tuple-element.20.refs_1_), channel_id=1, source_target_pairs={{32,0},{64,32},{96,64},{0,96},{33,1},{65,33},{97,65},{1,97},{34,2}... | collective-permute-start | bytes 884744 | tf_op jit(solution)/shard_map/ppermute | solution.py:425
  42.3 9.3 %collective-permute-start.2 = (bf16[4,144,128]{2,1,0:T(8,128)(2,1)S(1)}, bf16[4,144,128]{2,1,0:T(8,128)(2,1)S(1)}, u32[]{:S(2)}, u32[]{:S(2)}) collective-permute-start(bf16[4,144,128]{2,1,0:T(8,128)(2,1)S(1)} %slice.9), channel_id=1, source_target_pairs={{64,0},{96,32},{0,64},{32,96},{65,1},{97,33},{1,65},{33,97},{66,2}... | collective-permute-start | bytes 442376 | tf_op jit(solution)/shard_map/ppermute | solution.py:425
  45.4 7.4 %collective-permute-start.3 = (bf16[4,144,128]{2,1,0:T(8,128)(2,1)S(1)}, bf16[4,144,128]{2,1,0:T(8,128)(2,1)S(1)}, u32[]{:S(2)}, u32[]{:S(2)}) collective-permute-start(bf16[4,144,128]{2,1,0:T(8,128)(2,1)S(1)} %slice.12), channel_id=1, source_target_pairs={{96,0},{0,32},{32,64},{64,96},{97,1},{1,33},{33,65},{65,97},{98,2}... | collective-permute-start | bytes 442376 | tf_op jit(solution)/shard_map/ppermute | solution.py:425
  91.3 24.5 %copy-start = (bf16[432,384]{1,0:T(8,128)(2,1)S(1)}, bf16[432,384]{1,0:T(8,128)(2,1)}, u32[]{:S(2)}) copy-start(bf16[432,384]{1,0:T(8,128)(2,1)} %kernel.1) | copy-start | bytes 995332
  92.0 16.2 %all-to-all-start.4 = ((bf16[16,24,128]{2,1,0:T(8,128)(2,1)}), bf16[16,24,128]{2,1,0:T(8,128)(2,1)S(1)}, u32[]{:S(2)}, u32[]{:S(2)}) async-start(bf16[16,24,128]{2,1,0:T(8,128)(2,1)} %bitcast.8), calls=%async_computation.4 | async-start | bytes 196608 | tf_op jit(solution)/shard_map/all_to_all | solution.py:456
  108.3 7.5 %collective-permute-start.4 = (bf16[3,24,128]{2,1,0:T(8,128)(2,1)S(1)}, bf16[3,24,128]{2,1,0:T(8,128)(2,1)S(1)}, u32[]{:S(2)}, u32[]{:S(2)}) collective-permute-start(bf16[3,24,128]{2,1,0:T(8,128)(2,1)S(1)} %fusion.own), channel_id=1, source_target_pairs={{0,8},{1,9},{2,10},{3,11},{8,16},{9,17},{10,18},{11,19},{16,24},{1... | collective-permute-start | bytes 55304 | tf_op jit(solution)/shard_map/ppermute | solution.py:430
  110.2 0.7 copy-start.1
